TPU v7x, 512 devices: a whole 4x4x16 slice. The times are simulated.
512 devices in a mesh: row: 64 (over y_lo, z, core), col: 8 (over x, y_hi).
Axes of the slice: x: 4, y: 4 (y_hi: 2, y_lo: 2; y = y_hi * 2 + y_lo), z: 16, core: 2. Of those that a mesh axis runs over, the one named last changes fastest.
Arguments:
- x_tiles: bfloat16 [192, 32, 128, 128], P('row', 'col'), may hold values from -0.59765625 to 0.59765625
- tile_cols: int32 [192, 32], P('row', 'col'), may hold values from 0 to 191, as said below
- tile_counts: int32 [192, 8], P('row', 'col'), may hold values from 1 to 4
Outputs:
- product: bfloat16 [192, 32, 128, 128], P('row', 'col')
Inputs may be any that keep to these rules, and one draw needn't show every extreme that they name: `tile_cols`: in block row i the slots p * 4 to (p + 1) * 4 - 1 hold 4 distinct block columns of panel p, each of the form p * 24 + ((i + d) mod 24) with -2 <= d <= 2.
All inputs are finite; a program needn't handle non-finite values.
Results may differ from a plain program's by a relative error of at most 0.001.
Values may be sent and summed in bfloat16 or wider, within the bound.
No kernel may reach another device: no remote copies, remote signals or barrier semaphores. Data moves between devices by JAX's collectives and lax.ppermute only.
A program may use at most 128 MiB of HBM per device.

v0:
```python
import jax
import jax.numpy as jnp
from jax import lax
from jax.sharding import PartitionSpec as P

PANELS = 8
PS = 4


def from_behind(block, axis, distance):
    devices = range(lax.axis_size(axis))
    route = [((i - distance) % len(devices), i) for i in devices]
    return lax.ppermute(block, axis, route)


def slot_live(tile_cols, tile_counts):
    repeated = jnp.repeat(tile_counts, PS, axis=1)
    position = lax.broadcasted_iota(jnp.int32, tile_cols.shape, 1) % PS
    return position < repeated


def body(x_tiles, tile_cols, tile_counts):
    rows_here = tile_cols.shape[0]
    count_row = lax.axis_size("row")
    here = lax.axis_index("row")
    stride = count_row // PANELS
    zero_tile = jnp.zeros((), x_tiles.dtype)
    own_live = slot_live(tile_cols, tile_counts)
    left_tiles, left_cols, left_counts = (
        lax.all_gather(x_tiles, "col", axis=1, tiled=True),
        lax.all_gather(tile_cols, "col", axis=1, tiled=True),
        lax.all_gather(tile_counts, "col", axis=1, tiled=True),
    )
    left_keyed = jnp.where(slot_live(left_cols, left_counts), left_cols, -1).astype(jnp.int32)
    block = (x_tiles, tile_cols, tile_counts)
    local_span = jnp.arange(rows_here, dtype=jnp.int32)
    offsets = sorted(
        set(((p * stride + e) % count_row for p in range(PANELS) for e in (-1, 0, 1))) - {0}
    )
    pieces = [block]
    id_list = [here * rows_here + local_span]
    for offset in offsets:
        moved = from_behind((block[0], block[1], block[2]), "row", count_row - offset)
        pieces.append(moved)
        id_list.append((here + offset) % count_row * rows_here + local_span)
    stack_tiles = jnp.concatenate([piece[0] for piece in pieces], axis=0)
    stack_cols = jnp.concatenate([piece[1] for piece in pieces], axis=0)
    stack_counts = jnp.concatenate([piece[2] for piece in pieces], axis=0)
    stack_ids = jnp.concatenate(id_list, axis=0).astype(jnp.int32)
    stack_keyed = jnp.where(slot_live(stack_cols, stack_counts), stack_cols, -1).astype(jnp.int32)
    position = jnp.arange(stack_ids.shape[0], dtype=jnp.int32)
    earlier = (stack_ids[:, None] == stack_ids[None, :]) & (position[:, None] > position[None, :])
    unique_row = jnp.logical_not(jnp.any(earlier, axis=1))
    group = 2 * PS
    turns = left_cols.shape[1] // group

    def advance(accum, index):
        first = index * group
        part_tiles = lax.dynamic_slice_in_dim(left_tiles, first, group, 1)
        part_keyed = lax.dynamic_slice_in_dim(left_keyed, first, group, 1)
        part_tiles = jnp.where((part_keyed >= 0)[:, :, None, None], part_tiles, zero_tile)
        matches = (part_keyed[:, :, None] == stack_ids[None, None, :]) & unique_row[None, None, :]
        chosen = jnp.einsum(
            "rgf,fuxy->rguxy",
            matches.astype(jnp.bfloat16),
            stack_tiles,
            preferred_element_type=jnp.float32,
        ).astype(jnp.bfloat16)
        chosen_cols = jnp.sum(
            jnp.where(matches[:, :, :, None], stack_keyed[None, None, :, :], 0), axis=2
        )
        hits = (chosen_cols[:, :, :, None] == tile_cols[:, None, None, :]).astype(jnp.bfloat16)
        placed = jnp.einsum(
            "rgus,rguxy->rgsxy", hits, chosen, preferred_element_type=jnp.float32
        ).astype(jnp.bfloat16)
        accum = accum + jnp.einsum(
            "rgxy,rgsyz->rsxz", part_tiles, placed, preferred_element_type=jnp.float32
        )
        return (accum, None)

    initial = jnp.zeros(
        (rows_here, tile_cols.shape[1], x_tiles.shape[-1], x_tiles.shape[-1]), jnp.float32
    )
    summed, _ = lax.scan(advance, initial, jnp.arange(turns, dtype=jnp.int32))
    return jnp.where(own_live[:, :, None, None], summed, 0.0).astype(jnp.bfloat16)


def solution(mesh):
    placed = (P("row", "col", None, None), P("row", "col"), P("row", "col"))
    return jax.shard_map(
        body, mesh=mesh, in_specs=placed, out_specs=P("row", "col", None, None), check_vma=False
    )
```

profile of v0, /device:TPU:80, one launch (start us, length us, event | category | flops | bytes accessed | tf_op | source)
XLA Modules:
  0.0 1222.7 jit_solution(1086816939266158125)
XLA Ops:
  9.2 11.8 collective-permute-start.1
  45.3 45.1 %collective-permute-done.12 = s32[3,1]{0,1:T(1,128)S(1)} collective-permute-done((s32[3,1]{0,1:T(1,128)}, s32[3,1]{0,1:T(1,128)S(1)}, u32[]{:S(2)}, u32[]{:S(2)}) %collective-permute-start.12) | collective-permute-done | bytes 44 | tf_op jit(solution)/shard_map/ppermute | solution.py:13
  117.9 11.5 collective-permute-start.17
  129.4 11.3 collective-permute-start.18
  378.7 27.4 %collective-permute-done.49 = bf16[3,4,128,128]{3,0,2,1:T(4,128)(2,1)S(1)} collective-permute-done((bf16[3,4,128,128]{3,0,2,1:T(4,128)(2,1)S(1)}, bf16[3,4,128,128]{3,0,2,1:T(4,128)(2,1)S(1)}, u32[]{:S(2)}, u32[]{:S(2)}) %collective-permute-start.49) | collective-permute-done | bytes 393248 | tf_op jit(solution)/shard_map/ppermute | solution.py:13
  408.0 48.2 %collective-permute-done.50 = bf16[3,4,128,128]{3,0,2,1:T(4,128)(2,1)S(1)} collective-permute-done((bf16[3,4,128,128]{3,0,2,1:T(4,128)(2,1)S(1)}, bf16[3,4,128,128]{3,0,2,1:T(4,128)(2,1)S(1)}, u32[]{:S(2)}, u32[]{:S(2)}) %collective-permute-start.50) | collective-permute-done | bytes 393248 | tf_op jit(solution)/shard_map/ppermute | solution.py:13
  456.2 22.4 %collective-permute-start.55 = (bf16[3,4,128,128]{3,0,2,1:T(4,128)(2,1)S(1)}, bf16[3,4,128,128]{3,0,2,1:T(4,128)(2,1)}, u32[]{:S(2)}, u32[]{:S(2)}) collective-permute-start(bf16[3,4,128,128]{3,0,2,1:T(4,128)(2,1)S(1)} %copy.170), channel_id=1, source_target_pairs={{200,0},{208,8},{216,16},{224,24},{232,32},{240,40},{248,48},{256,... | collective-permute-start | bytes 1179656 | tf_op jit(solution)/shard_map/ppermute | solution.py:13
  480.6 29.5 %collective-permute-done.52 = bf16[3,4,128,128]{3,0,2,1:T(4,128)(2,1)S(1)} collective-permute-done((bf16[3,4,128,128]{3,0,2,1:T(4,128)(2,1)S(1)}, bf16[3,4,128,128]{3,0,2,1:T(4,128)(2,1)S(1)}, u32[]{:S(2)}, u32[]{:S(2)}) %collective-permute-start.52) | collective-permute-done | bytes 393248 | tf_op jit(solution)/shard_map/ppermute | solution.py:13
  512.0 38.5 %collective-permute-done.53 = bf16[3,4,128,128]{3,0,2,1:T(4,128)(2,1)S(1)} collective-permute-done((bf16[3,4,128,128]{3,0,2,1:T(4,128)(2,1)S(1)}, bf16[3,4,128,128]{3,0,2,1:T(4,128)(2,1)S(1)}, u32[]{:S(2)}, u32[]{:S(2)}) %collective-permute-start.53) | collective-permute-done | bytes 393248 | tf_op jit(solution)/shard_map/ppermute | solution.py:13
  550.5 52.7 %collective-permute-start.58 = (bf16[3,4,128,128]{3,0,2,1:T(4,128)(2,1)S(1)}, bf16[3,4,128,128]{3,0,2,1:T(4,128)(2,1)}, u32[]{:S(2)}, u32[]{:S(2)}) collective-permute-start(bf16[3,4,128,128]{3,0,2,1:T(4,128)(2,1)S(1)} %copy.170), channel_id=1, source_target_pairs={{264,0},{272,8},{280,16},{288,24},{296,32},{304,40},{312,48},{320,... | collective-permute-start | bytes 1179656 | tf_op jit(solution)/shard_map/ppermute | solution.py:13
  603.8 18.3 %all-gather = s32[8,1,3]{2,1,0:T(1,128)S(1)} all-gather(s32[1,1,3]{2,1,0:T(1,128)} %bitcast.55), channel_id=1, replica_groups=mesh['row'=64,'col'=8] {'col'}, dimensions={0}, use_global_device_ids=true | all-gather | bytes 108 | tf_op jit(solution)/shard_map/all_gather | solution.py:32
  623.9 30.9 %all-gather.1 = s32[8,4,3]{2,1,0:T(4,128)S(1)} all-gather(s32[1,4,3]{2,1,0:T(4,128)S(1)} %bitcast.53), channel_id=1, replica_groups=mesh['row'=64,'col'=8] {'col'}, dimensions={0}, use_global_device_ids=true | all-gather | bytes 432 | tf_op jit(solution)/shard_map/all_gather | solution.py:31
  663.8 19.7 %collective-permute-start.61 = (bf16[3,4,128,128]{3,0,2,1:T(4,128)(2,1)S(1)}, bf16[3,4,128,128]{3,0,2,1:T(4,128)(2,1)S(1)}, u32[]{:S(2)}, u32[]{:S(2)}) collective-permute-start(bf16[3,4,128,128]{3,0,2,1:T(4,128)(2,1)S(1)} %copy.170), channel_id=1, source_target_pairs={{328,0},{336,8},{344,16},{352,24},{360,32},{368,40},{376,48},{384,... | collective-permute-start | bytes 1179656 | tf_op jit(solution)/shard_map/ppermute | solution.py:13
  687.7 42.4 %collective-permute-done.59 = bf16[3,4,128,128]{3,0,2,1:T(4,128)(2,1)S(1)} collective-permute-done((bf16[3,4,128,128]{3,0,2,1:T(4,128)(2,1)S(1)}, bf16[3,4,128,128]{3,0,2,1:T(4,128)(2,1)S(1)}, u32[]{:S(2)}, u32[]{:S(2)}) %collective-permute-start.59) | collective-permute-done | bytes 393248 | tf_op jit(solution)/shard_map/ppermute | solution.py:13
  730.1 11.8 collective-permute-start.64
  741.9 16.8 %collective-permute-start.65 = (bf16[3,4,128,128]{3,0,2,1:T(4,128)(2,1)S(1)}, bf16[3,4,128,128]{3,0,2,1:T(4,128)(2,1)}, u32[]{:S(2)}, u32[]{:S(2)}) collective-permute-start(bf16[3,4,128,128]{3,0,2,1:T(4,128)(2,1)S(1)} %copy.170), channel_id=1, source_target_pairs={{440,0},{448,8},{456,16},{464,24},{472,32},{480,40},{488,48},{496,... | collective-permute-start | bytes 1179656 | tf_op jit(solution)/shard_map/ppermute | solution.py:13
  758.7 19.6 %collective-permute-done.61 = bf16[3,4,128,128]{3,0,2,1:T(4,128)(2,1)S(1)} collective-permute-done((bf16[3,4,128,128]{3,0,2,1:T(4,128)(2,1)S(1)}, bf16[3,4,128,128]{3,0,2,1:T(4,128)(2,1)S(1)}, u32[]{:S(2)}, u32[]{:S(2)}) %collective-permute-start.61) | collective-permute-done | bytes 393248 | tf_op jit(solution)/shard_map/ppermute | solution.py:13
  778.3 76.2 %collective-permute-start.66 = (bf16[3,4,128,128]{3,0,2,1:T(4,128)(2,1)S(1)}, bf16[3,4,128,128]{3,0,2,1:T(4,128)(2,1)}, u32[]{:S(2)}, u32[]{:S(2)}) collective-permute-start(bf16[3,4,128,128]{3,0,2,1:T(4,128)(2,1)S(1)} %copy.170), channel_id=1, source_target_pairs={{448,0},{456,8},{464,16},{472,24},{480,32},{488,40},{496,48},{504,... | collective-permute-start | bytes 1179656 | tf_op jit(solution)/shard_map/ppermute | solution.py:13
  854.6 60.5 %collective-permute-start.67 = (bf16[3,4,128,128]{3,0,2,1:T(4,128)(2,1)S(1)}, bf16[3,4,128,128]{3,0,2,1:T(4,128)(2,1)}, u32[]{:S(2)}, u32[]{:S(2)}) collective-permute-start(bf16[3,4,128,128]{3,0,2,1:T(4,128)(2,1)S(1)} %copy.170), channel_id=1, source_target_pairs={{456,0},{464,8},{472,16},{480,24},{488,32},{496,40},{504,48},{0,56... | collective-permute-start | bytes 1179656 | tf_op jit(solution)/shard_map/ppermute | solution.py:13
  919.2 13.1 %collective-permute-done.66 = bf16[3,4,128,128]{3,0,2,1:T(4,128)(2,1)} collective-permute-done((bf16[3,4,128,128]{3,0,2,1:T(4,128)(2,1)S(1)}, bf16[3,4,128,128]{3,0,2,1:T(4,128)(2,1)}, u32[]{:S(2)}, u32[]{:S(2)}) %collective-permute-start.66) | collective-permute-done | bytes 393248 | tf_op jit(solution)/shard_map/ppermute | solution.py:13
  932.4 21.8 %collective-permute-done.67 = bf16[3,4,128,128]{3,0,2,1:T(4,128)(2,1)} collective-permute-done((bf16[3,4,128,128]{3,0,2,1:T(4,128)(2,1)S(1)}, bf16[3,4,128,128]{3,0,2,1:T(4,128)(2,1)}, u32[]{:S(2)}, u32[]{:S(2)}) %collective-permute-start.67) | collective-permute-done | bytes 393248 | tf_op jit(solution)/shard_map/ppermute | solution.py:13
  954.2 28.1 %collective-permute-done.68 = bf16[3,4,128,128]{3,0,2,1:T(4,128)(2,1)} collective-permute-done((bf16[3,4,128,128]{3,0,2,1:T(4,128)(2,1)S(1)}, bf16[3,4,128,128]{3,0,2,1:T(4,128)(2,1)}, u32[]{:S(2)}, u32[]{:S(2)}) %collective-permute-start.68) | collective-permute-done | bytes 393248 | tf_op jit(solution)/shard_map/ppermute | solution.py:13
  982.3 153.6 %concatenate.18 = bf16[72,4,128,128]{3,0,2,1:T(8,128)(2,1)} concatenate(bf16[3,4,128,128]{3,0,2,1:T(4,128)(2,1)S(1)} %copy.170, bf16[3,4,128,128]{3,0,2,1:T(4,128)(2,1)S(1)} %collective-permute-done.46, bf16[3,4,128,128]{3,0,2,1:T(4,128)(2,1)S(1)} %collective-permute-done.47, bf16[3,4,128,128]{3,0,2,1:T(4,128)(2,1)S(1)} %collective-permute-done.48, ...), dimensions={0} | concatenate | bytes 18874368 | tf_op jit(solution)/shard_map/concatenate | solution.py:46
  1135.8 78.9 %while.11 = (s32[]{:T(128)}, f32[3,4,128,128]{2,3,1,0:T(8,128)S(1)}, s32[4]{0:T(128)S(1)}, s32[3,32]{1,0:T(4,128)S(1)}, s32[72]{0:T(128)S(1)}, /*index=5*/pred[7...) while((s32[]{:T(128)}, ...), condition=%wide.region_3.4_spmd.clone, body=%wide.region_1.3_spmd.clone.sunk | while | flops 645681728 | bytes 24386944 | solution.py:84
  (254 shorter events, 394.0 us)
Async XLA Ops:
  6.5 1129.3 %all-gather.4.cloned.1.call-start = ((), (), s32[]{:S(2)}) async-start(), calls=%async_computation | async-start | bytes 3538944 | tf_op jit(solution)/shard_map/all_gather | solution.py:30
  22.3 335.0 %collective-permute-start.46 = (bf16[3,4,128,128]{3,0,2,1:T(4,128)(2,1)S(1)}, bf16[3,4,128,128]{3,0,2,1:T(4,128)(2,1)S(1)}, u32[]{:S(2)}, u32[]{:S(2)}) collective-permute-start(bf16[3,4,128,128]{3,0,2,1:T(4,128)(2,1)S(1)} %copy.170), channel_id=1, source_target_pairs={{8,0},{16,8},{24,16},{32,24},{40,32},{48,40},{56,48},{64,56},{72,6... | collective-permute-start | bytes 1179656 | tf_op jit(solution)/shard_map/ppermute | solution.py:13
  24.8 340.8 %collective-permute-start.47 = (bf16[3,4,128,128]{3,0,2,1:T(4,128)(2,1)S(1)}, bf16[3,4,128,128]{3,0,2,1:T(4,128)(2,1)S(1)}, u32[]{:S(2)}, u32[]{:S(2)}) collective-permute-start(bf16[3,4,128,128]{3,0,2,1:T(4,128)(2,1)S(1)} %copy.170), channel_id=1, source_target_pairs={{56,0},{64,8},{72,16},{80,24},{88,32},{96,40},{104,48},{112,56},{1... | collective-permute-start | bytes 1179656 | tf_op jit(solution)/shard_map/ppermute | solution.py:13
  29.8 340.9 %collective-permute-start.48 = (bf16[3,4,128,128]{3,0,2,1:T(4,128)(2,1)S(1)}, bf16[3,4,128,128]{3,0,2,1:T(4,128)(2,1)S(1)}, u32[]{:S(2)}, u32[]{:S(2)}) collective-permute-start(bf16[3,4,128,128]{3,0,2,1:T(4,128)(2,1)S(1)} %copy.170), channel_id=1, source_target_pairs={{64,0},{72,8},{80,16},{88,24},{96,32},{104,40},{112,48},{120,56},{... | collective-permute-start | bytes 1179656 | tf_op jit(solution)/shard_map/ppermute | solution.py:13
  43.4 61.8 %collective-permute-start.13 = (s32[3,1]{0,1:T(1,128)}, s32[3,1]{0,1:T(1,128)S(1)}, u32[]{:S(2)}, u32[]{:S(2)}) collective-permute-start(s32[3,1]{0,1:T(1,128)} %param.7), channel_id=1, source_target_pairs={{312,0},{320,8},{328,16},{336,24},{344,32},{352,40},{360,48},{368,... | collective-permute-start | bytes 44 | tf_op jit(solution)/shard_map/ppermute | solution.py:13
  348.6 107.7 %collective-permute-start.50 = (bf16[3,4,128,128]{3,0,2,1:T(4,128)(2,1)S(1)}, bf16[3,4,128,128]{3,0,2,1:T(4,128)(2,1)S(1)}, u32[]{:S(2)}, u32[]{:S(2)}) collective-permute-start(bf16[3,4,128,128]{3,0,2,1:T(4,128)(2,1)S(1)} %copy.170), channel_id=1, source_target_pairs={{120,0},{128,8},{136,16},{144,24},{152,32},{160,40},{168,48},{176,... | collective-permute-start | bytes 1179656 | tf_op jit(solution)/shard_map/ppermute | solution.py:13
  357.3 121.4 %collective-permute-start.51 = (bf16[3,4,128,128]{3,0,2,1:T(4,128)(2,1)S(1)}, bf16[3,4,128,128]{3,0,2,1:T(4,128)(2,1)S(1)}, u32[]{:S(2)}, u32[]{:S(2)}) collective-permute-start(bf16[3,4,128,128]{3,0,2,1:T(4,128)(2,1)S(1)} %copy.170), channel_id=1, source_target_pairs={{128,0},{136,8},{144,16},{152,24},{160,32},{168,40},{176,48},{184,... | collective-permute-start | bytes 1179656 | tf_op jit(solution)/shard_map/ppermute | solution.py:13
  365.6 144.4 %collective-permute-start.52 = (bf16[3,4,128,128]{3,0,2,1:T(4,128)(2,1)S(1)}, bf16[3,4,128,128]{3,0,2,1:T(4,128)(2,1)S(1)}, u32[]{:S(2)}, u32[]{:S(2)}) collective-permute-start(bf16[3,4,128,128]{3,0,2,1:T(4,128)(2,1)S(1)} %copy.170), channel_id=1, source_target_pairs={{136,0},{144,8},{152,16},{160,24},{168,32},{176,40},{184,48},{192,... | collective-permute-start | bytes 1179656 | tf_op jit(solution)/shard_map/ppermute | solution.py:13
  370.7 179.7 %collective-permute-start.53 = (bf16[3,4,128,128]{3,0,2,1:T(4,128)(2,1)S(1)}, bf16[3,4,128,128]{3,0,2,1:T(4,128)(2,1)S(1)}, u32[]{:S(2)}, u32[]{:S(2)}) collective-permute-start(bf16[3,4,128,128]{3,0,2,1:T(4,128)(2,1)S(1)} %copy.170), channel_id=1, source_target_pairs={{184,0},{192,8},{200,16},{208,24},{216,32},{224,40},{232,48},{240,... | collective-permute-start | bytes 1179656 | tf_op jit(solution)/shard_map/ppermute | solution.py:13
  406.1 248.9 %collective-permute-start.54 = (bf16[3,4,128,128]{3,0,2,1:T(4,128)(2,1)S(1)}, bf16[3,4,128,128]{3,0,2,1:T(4,128)(2,1)}, u32[]{:S(2)}, u32[]{:S(2)}) collective-permute-start(bf16[3,4,128,128]{3,0,2,1:T(4,128)(2,1)S(1)} %copy.170), channel_id=1, source_target_pairs={{192,0},{200,8},{208,16},{216,24},{224,32},{232,40},{240,48},{248,... | collective-permute-start | bytes 1179656 | tf_op jit(solution)/shard_map/ppermute | solution.py:13
  456.2 200.8 %collective-permute-start.55 = (bf16[3,4,128,128]{3,0,2,1:T(4,128)(2,1)S(1)}, bf16[3,4,128,128]{3,0,2,1:T(4,128)(2,1)}, u32[]{:S(2)}, u32[]{:S(2)}) collective-permute-start(bf16[3,4,128,128]{3,0,2,1:T(4,128)(2,1)S(1)} %copy.170), channel_id=1, source_target_pairs={{200,0},{208,8},{216,16},{224,24},{232,32},{240,40},{248,48},{256,... | collective-permute-start | bytes 1179656 | tf_op jit(solution)/shard_map/ppermute | solution.py:13
  478.7 185.1 %collective-permute-start.56 = (bf16[3,4,128,128]{3,0,2,1:T(4,128)(2,1)S(1)}, bf16[3,4,128,128]{3,0,2,1:T(4,128)(2,1)}, u32[]{:S(2)}, u32[]{:S(2)}) collective-permute-start(bf16[3,4,128,128]{3,0,2,1:T(4,128)(2,1)S(1)} %copy.170), channel_id=1, source_target_pairs={{248,0},{256,8},{264,16},{272,24},{280,32},{288,40},{296,48},{304,... | collective-permute-start | bytes 1179656 | tf_op jit(solution)/shard_map/ppermute | solution.py:13
  510.1 173.4 %collective-permute-start.57 = (bf16[3,4,128,128]{3,0,2,1:T(4,128)(2,1)S(1)}, bf16[3,4,128,128]{3,0,2,1:T(4,128)(2,1)}, u32[]{:S(2)}, u32[]{:S(2)}) collective-permute-start(bf16[3,4,128,128]{3,0,2,1:T(4,128)(2,1)S(1)} %copy.170), channel_id=1, source_target_pairs={{256,0},{264,8},{272,16},{280,24},{288,32},{296,40},{304,48},{312,... | collective-permute-start | bytes 1179656 | tf_op jit(solution)/shard_map/ppermute | solution.py:13
  550.5 135.0 %collective-permute-start.58 = (bf16[3,4,128,128]{3,0,2,1:T(4,128)(2,1)S(1)}, bf16[3,4,128,128]{3,0,2,1:T(4,128)(2,1)}, u32[]{:S(2)}, u32[]{:S(2)}) collective-permute-start(bf16[3,4,128,128]{3,0,2,1:T(4,128)(2,1)S(1)} %copy.170), channel_id=1, source_target_pairs={{264,0},{272,8},{280,16},{288,24},{296,32},{304,40},{312,48},{320,... | collective-permute-start | bytes 1179656 | tf_op jit(solution)/shard_map/ppermute | solution.py:13
  655.1 75.0 %collective-permute-start.59 = (bf16[3,4,128,128]{3,0,2,1:T(4,128)(2,1)S(1)}, bf16[3,4,128,128]{3,0,2,1:T(4,128)(2,1)S(1)}, u32[]{:S(2)}, u32[]{:S(2)}) collective-permute-start(bf16[3,4,128,128]{3,0,2,1:T(4,128)(2,1)S(1)} %copy.170), channel_id=1, source_target_pairs={{312,0},{320,8},{328,16},{336,24},{344,32},{352,40},{360,48},{368,... | collective-permute-start | bytes 1179656 | tf_op jit(solution)/shard_map/ppermute | solution.py:13
  657.0 84.9 %collective-permute-start.60 = (bf16[3,4,128,128]{3,0,2,1:T(4,128)(2,1)S(1)}, bf16[3,4,128,128]{3,0,2,1:T(4,128)(2,1)S(1)}, u32[]{:S(2)}, u32[]{:S(2)}) collective-permute-start(bf16[3,4,128,128]{3,0,2,1:T(4,128)(2,1)S(1)} %copy.170), channel_id=1, source_target_pairs={{320,0},{328,8},{336,16},{344,24},{352,32},{360,40},{368,48},{376,... | collective-permute-start | bytes 1179656 | tf_op jit(solution)/shard_map/ppermute | solution.py:13
  663.8 114.5 %collective-permute-start.61 = (bf16[3,4,128,128]{3,0,2,1:T(4,128)(2,1)S(1)}, bf16[3,4,128,128]{3,0,2,1:T(4,128)(2,1)S(1)}, u32[]{:S(2)}, u32[]{:S(2)}) collective-permute-start(bf16[3,4,128,128]{3,0,2,1:T(4,128)(2,1)S(1)} %copy.170), channel_id=1, source_target_pairs={{328,0},{336,8},{344,16},{352,24},{360,32},{368,40},{376,48},{384,... | collective-permute-start | bytes 1179656 | tf_op jit(solution)/shard_map/ppermute | solution.py:13
  683.5 171.0 %collective-permute-start.62 = (bf16[3,4,128,128]{3,0,2,1:T(4,128)(2,1)S(1)}, bf16[3,4,128,128]{3,0,2,1:T(4,128)(2,1)S(1)}, u32[]{:S(2)}, u32[]{:S(2)}) collective-permute-start(bf16[3,4,128,128]{3,0,2,1:T(4,128)(2,1)S(1)} %copy.170), channel_id=1, source_target_pairs={{376,0},{384,8},{392,16},{400,24},{408,32},{416,40},{424,48},{432,... | collective-permute-start | bytes 1179656 | tf_op jit(solution)/shard_map/ppermute | solution.py:13
  685.4 229.6 %collective-permute-start.63 = (bf16[3,4,128,128]{3,0,2,1:T(4,128)(2,1)S(1)}, bf16[3,4,128,128]{3,0,2,1:T(4,128)(2,1)S(1)}, u32[]{:S(2)}, u32[]{:S(2)}) collective-permute-start(bf16[3,4,128,128]{3,0,2,1:T(4,128)(2,1)S(1)} %copy.170), channel_id=1, source_target_pairs={{384,0},{392,8},{400,16},{408,24},{416,32},{424,40},{432,48},{440,... | collective-permute-start | bytes 1179656 | tf_op jit(solution)/shard_map/ppermute | solution.py:13
  730.1 189.1 %collective-permute-start.64 = (bf16[3,4,128,128]{3,0,2,1:T(4,128)(2,1)S(1)}, bf16[3,4,128,128]{3,0,2,1:T(4,128)(2,1)}, u32[]{:S(2)}, u32[]{:S(2)}) collective-permute-start(bf16[3,4,128,128]{3,0,2,1:T(4,128)(2,1)S(1)} %copy.170), channel_id=1, source_target_pairs={{392,0},{400,8},{408,16},{416,24},{424,32},{432,40},{440,48},{448,... | collective-permute-start | bytes 1179656 | tf_op jit(solution)/shard_map/ppermute | solution.py:13
  741.9 177.3 %collective-permute-start.65 = (bf16[3,4,128,128]{3,0,2,1:T(4,128)(2,1)S(1)}, bf16[3,4,128,128]{3,0,2,1:T(4,128)(2,1)}, u32[]{:S(2)}, u32[]{:S(2)}) collective-permute-start(bf16[3,4,128,128]{3,0,2,1:T(4,128)(2,1)S(1)} %copy.170), channel_id=1, source_target_pairs={{440,0},{448,8},{456,16},{464,24},{472,32},{480,40},{488,48},{496,... | collective-permute-start | bytes 1179656 | tf_op jit(solution)/shard_map/ppermute | solution.py:13
  778.3 154.0 %collective-permute-start.66 = (bf16[3,4,128,128]{3,0,2,1:T(4,128)(2,1)S(1)}, bf16[3,4,128,128]{3,0,2,1:T(4,128)(2,1)}, u32[]{:S(2)}, u32[]{:S(2)}) collective-permute-start(bf16[3,4,128,128]{3,0,2,1:T(4,128)(2,1)S(1)} %copy.170), channel_id=1, source_target_pairs={{448,0},{456,8},{464,16},{472,24},{480,32},{488,40},{496,48},{504,... | collective-permute-start | bytes 1179656 | tf_op jit(solution)/shard_map/ppermute | solution.py:13
  854.6 99.6 %collective-permute-start.67 = (bf16[3,4,128,128]{3,0,2,1:T(4,128)(2,1)S(1)}, bf16[3,4,128,128]{3,0,2,1:T(4,128)(2,1)}, u32[]{:S(2)}, u32[]{:S(2)}) collective-permute-start(bf16[3,4,128,128]{3,0,2,1:T(4,128)(2,1)S(1)} %copy.170), channel_id=1, source_target_pairs={{456,0},{464,8},{472,16},{480,24},{488,32},{496,40},{504,48},{0,56... | collective-permute-start | bytes 1179656 | tf_op jit(solution)/shard_map/ppermute | solution.py:13
  915.0 67.2 %collective-permute-start.68 = (bf16[3,4,128,128]{3,0,2,1:T(4,128)(2,1)S(1)}, bf16[3,4,128,128]{3,0,2,1:T(4,128)(2,1)}, u32[]{:S(2)}, u32[]{:S(2)}) collective-permute-start(bf16[3,4,128,128]{3,0,2,1:T(4,128)(2,1)S(1)} %copy.170), channel_id=1, source_target_pairs={{504,0},{0,8},{8,16},{16,24},{24,32},{32,40},{40,48},{48,56},{56,6... | collective-permute-start | bytes 1179656 | tf_op jit(solution)/shard_map/ppermute | solution.py:13
  (79 other events, 5576.6 us)
Sparse Core Ops, SparseCore 0:
  10.6 79.5 all-gather.3
where the time goes:
time: 1230 us; the launch traced here: 1220 us
  starting transfers between devices  563 us (46%)
  waiting for transfers between devices  352 us (29%)
  local copies, waits for them, and re-layouts  162 us (13%)
  matrix products  71.5 us (6%)
  blocking collectives  49.1 us (4%)
  between operations  15 us (1%)
    ppermute x69, starting transfers between devices, from_behind(): return lax.ppermute(block, axis, route)  563 us
    ppermute x69, waiting for transfers between devices, from_behind(): return lax.ppermute(block, axis, route)  351 us
    concatenate x1, local copies, waits for them, and re-layouts, body(): stack_tiles = jnp.concatenate([piece[0] for piece in pieces], axis=0)  154 us
    all_gather x1, blocking collectives, body(): lax.all_gather(tile_cols, 'col', axis=1, tiled=True)  30.9 us
    dot_general x4, matrix products, advance(): jnp.einsum('rgus,rguxy->rgsxy', hits, chosen, preferred_element_type=jnp....  30.8 us
    dot_general x4, matrix products, advance(): jnp.einsum('rgf,fuxy->rguxy', matches.astype(jnp.bfloat16), stack_tiles,...  27.2 us
  transfers between devices with their start and end apart: 70, of which 26 were waited for; matrix products, arithmetic and copies ran while one was open for 13% of the time, Pallas kernels for 0%

commit v1 on v0

--- a/solution.py
+++ b/solution.py
@@ -26,9 +26,15 @@
     stride = count_row // PANELS
     zero_tile = jnp.zeros((), x_tiles.dtype)
     own_live = slot_live(tile_cols, tile_counts)
+
+    def follow_the_vectors(frame_in):
+        r_now = jnp.stack([frame_in for _ in range(lax.axis_size("col"))])
+        item_now = lax.all_to_all(r_now, "col", 0, 0)
+        return jnp.concatenate(item_now, 1)
+
     left_tiles, left_cols, left_counts = (
         lax.all_gather(x_tiles, "col", axis=1, tiled=True),
-        lax.all_gather(tile_cols, "col", axis=1, tiled=True),
+        follow_the_vectors(tile_cols),
         lax.all_gather(tile_counts, "col", axis=1, tiled=True),
     )
     left_keyed = jnp.where(slot_live(left_cols, left_counts), left_cols, -1).astype(jnp.int32)

time: 1230 us -> 1200 us (0.976)
  the two profiles are of different devices: /device:TPU:80 before, /device:TPU:4 now
where the time goes in v1:
time: 1200 us; the launch traced here: 1190 us
  starting transfers between devices  505 us (42%)
  waiting for transfers between devices  401 us (33%)
  local copies, waits for them, and re-layouts  162 us (14%)
  matrix products  71.5 us (6%)
  blocking collectives  15.8 us (1%)
  between operations  14.6 us (1%)
    ppermute x69, starting transfers between devices, from_behind(): return lax.ppermute(block, axis, route)  498 us
    ppermute x69, waiting for transfers between devices, from_behind(): return lax.ppermute(block, axis, route)  400 us
    concatenate x1, local copies, waits for them, and re-layouts, body(): stack_tiles = jnp.concatenate([piece[0] for piece in pieces], axis=0)  153 us
    dot_general x4, matrix products, advance(): jnp.einsum('rgus,rguxy->rgsxy', hits, chosen, preferred_element_type=jnp....  30.8 us
    dot_general x4, matrix products, advance(): jnp.einsum('rgf,fuxy->rguxy', matches.astype(jnp.bfloat16), stack_tiles,...  27.1 us
  transfers between devices with their start and end apart: 71, of which 31 were waited for; matrix products, arithmetic and copies ran while one was open for 14% of the time, Pallas kernels for 0%

profile of v1, /device:TPU:4, one launch (start us, length us, event | category | flops | bytes accessed | tf_op | source)
XLA Modules:
  0.0 1185.4 jit_solution(4918011812133014722)
XLA Ops:
  7.3 11.9 %collective-permute-start = (s32[3,1]{0,1:T(1,128)}, s32[3,1]{0,1:T(1,128)S(1)}, u32[]{:S(2)}, u32[]{:S(2)}) collective-permute-start(s32[3,1]{0,1:T(1,128)} %param.7), channel_id=1, source_target_pairs={{8,0},{16,8},{24,16},{32,24},{40,32},{48,40},{56,48},{64,56},{72,6... | collective-permute-start | bytes 44 | tf_op jit(solution)/shard_map/ppermute | solution.py:13
  59.5 59.7 %collective-permute-done.12 = s32[3,1]{0,1:T(1,128)S(1)} collective-permute-done((s32[3,1]{0,1:T(1,128)}, s32[3,1]{0,1:T(1,128)S(1)}, u32[]{:S(2)}, u32[]{:S(2)}) %collective-permute-start.12) | collective-permute-done | bytes 44 | tf_op jit(solution)/shard_map/ppermute | solution.py:13
  142.1 9.2 collective-permute-start.18
  188.8 9.0 collective-permute-start.5
  246.4 8.0 collective-permute-start.28
  358.9 8.9 collective-permute-start.51
  380.7 28.6 %collective-permute-done.49 = bf16[3,4,128,128]{3,0,2,1:T(4,128)(2,1)S(1)} collective-permute-done((bf16[3,4,128,128]{3,0,2,1:T(4,128)(2,1)S(1)}, bf16[3,4,128,128]{3,0,2,1:T(4,128)(2,1)S(1)}, u32[]{:S(2)}, u32[]{:S(2)}) %collective-permute-start.49) | collective-permute-done | bytes 393248 | tf_op jit(solution)/shard_map/ppermute | solution.py:13
  414.4 55.7 %collective-permute-done.50 = bf16[3,4,128,128]{3,0,2,1:T(4,128)(2,1)S(1)} collective-permute-done((bf16[3,4,128,128]{3,0,2,1:T(4,128)(2,1)S(1)}, bf16[3,4,128,128]{3,0,2,1:T(4,128)(2,1)S(1)}, u32[]{:S(2)}, u32[]{:S(2)}) %collective-permute-start.50) | collective-permute-done | bytes 393248 | tf_op jit(solution)/shard_map/ppermute | solution.py:13
  474.0 13.5 %collective-permute-done.52 = bf16[3,4,128,128]{3,0,2,1:T(4,128)(2,1)S(1)} collective-permute-done((bf16[3,4,128,128]{3,0,2,1:T(4,128)(2,1)S(1)}, bf16[3,4,128,128]{3,0,2,1:T(4,128)(2,1)S(1)}, u32[]{:S(2)}, u32[]{:S(2)}) %collective-permute-start.52) | collective-permute-done | bytes 393248 | tf_op jit(solution)/shard_map/ppermute | solution.py:13
  490.8 39.0 %collective-permute-done.53 = bf16[3,4,128,128]{3,0,2,1:T(4,128)(2,1)S(1)} collective-permute-done((bf16[3,4,128,128]{3,0,2,1:T(4,128)(2,1)S(1)}, bf16[3,4,128,128]{3,0,2,1:T(4,128)(2,1)S(1)}, u32[]{:S(2)}, u32[]{:S(2)}) %collective-permute-start.53) | collective-permute-done | bytes 393248 | tf_op jit(solution)/shard_map/ppermute | solution.py:13
  529.8 58.1 %collective-permute-start.58 = (bf16[3,4,128,128]{3,0,2,1:T(4,128)(2,1)S(1)}, bf16[3,4,128,128]{3,0,2,1:T(4,128)(2,1)}, u32[]{:S(2)}, u32[]{:S(2)}) collective-permute-start(bf16[3,4,128,128]{3,0,2,1:T(4,128)(2,1)S(1)} %copy.164), channel_id=1, source_target_pairs={{264,0},{272,8},{280,16},{288,24},{296,32},{304,40},{312,48},{320,... | collective-permute-start | bytes 1179656 | tf_op jit(solution)/shard_map/ppermute | solution.py:13
  588.7 15.8 %all-gather = s32[8,1,3]{2,1,0:T(1,128)S(1)} all-gather(s32[1,1,3]{2,1,0:T(1,128)} %bitcast.49), channel_id=1, replica_groups=mesh['row'=64,'col'=8] {'col'}, dimensions={0}, use_global_device_ids=true | all-gather | bytes 108 | tf_op jit(solution)/shard_map/all_gather | solution.py:38
  607.8 13.1 %collective-permute-done.55 = bf16[3,4,128,128]{3,0,2,1:T(4,128)(2,1)} collective-permute-done((bf16[3,4,128,128]{3,0,2,1:T(4,128)(2,1)S(1)}, bf16[3,4,128,128]{3,0,2,1:T(4,128)(2,1)}, u32[]{:S(2)}, u32[]{:S(2)}) %collective-permute-start.55) | collective-permute-done | bytes 393248 | tf_op jit(solution)/shard_map/ppermute | solution.py:13
  620.9 10.1 collective-permute-start.60
  648.8 10.4 collective-permute-start.63
  665.4 67.7 %collective-permute-done.60 = bf16[3,4,128,128]{3,0,2,1:T(4,128)(2,1)} collective-permute-done((bf16[3,4,128,128]{3,0,2,1:T(4,128)(2,1)S(1)}, bf16[3,4,128,128]{3,0,2,1:T(4,128)(2,1)}, u32[]{:S(2)}, u32[]{:S(2)}) %collective-permute-start.60) | collective-permute-done | bytes 393248 | tf_op jit(solution)/shard_map/ppermute | solution.py:13
  733.2 71.2 %collective-permute-start.65 = (bf16[3,4,128,128]{3,0,2,1:T(4,128)(2,1)S(1)}, bf16[3,4,128,128]{3,0,2,1:T(4,128)(2,1)}, u32[]{:S(2)}, u32[]{:S(2)}) collective-permute-start(bf16[3,4,128,128]{3,0,2,1:T(4,128)(2,1)S(1)} %copy.164), channel_id=1, source_target_pairs={{440,0},{448,8},{456,16},{464,24},{472,32},{480,40},{488,48},{496,... | collective-permute-start | bytes 1179656 | tf_op jit(solution)/shard_map/ppermute | solution.py:13
  816.4 16.9 %collective-permute-start.67 = (bf16[3,4,128,128]{3,0,2,1:T(4,128)(2,1)S(1)}, bf16[3,4,128,128]{3,0,2,1:T(4,128)(2,1)}, u32[]{:S(2)}, u32[]{:S(2)}) collective-permute-start(bf16[3,4,128,128]{3,0,2,1:T(4,128)(2,1)S(1)} %copy.164), channel_id=1, source_target_pairs={{456,0},{464,8},{472,16},{480,24},{488,32},{496,40},{504,48},{0,56... | collective-permute-start | bytes 1179656 | tf_op jit(solution)/shard_map/ppermute | solution.py:13
  833.3 28.1 %collective-permute-start.68 = (bf16[3,4,128,128]{3,0,2,1:T(4,128)(2,1)S(1)}, bf16[3,4,128,128]{3,0,2,1:T(4,128)(2,1)}, u32[]{:S(2)}, u32[]{:S(2)}) collective-permute-start(bf16[3,4,128,128]{3,0,2,1:T(4,128)(2,1)S(1)} %copy.164), channel_id=1, source_target_pairs={{504,0},{0,8},{8,16},{16,24},{24,32},{32,40},{40,48},{48,56},{56,6... | collective-permute-start | bytes 1179656 | tf_op jit(solution)/shard_map/ppermute | solution.py:13
  862.9 54.3 %collective-permute-done.66 = bf16[3,4,128,128]{3,0,2,1:T(4,128)(2,1)} collective-permute-done((bf16[3,4,128,128]{3,0,2,1:T(4,128)(2,1)S(1)}, bf16[3,4,128,128]{3,0,2,1:T(4,128)(2,1)}, u32[]{:S(2)}, u32[]{:S(2)}) %collective-permute-start.66) | collective-permute-done | bytes 393248 | tf_op jit(solution)/shard_map/ppermute | solution.py:13
  917.2 10.6 collective-permute-done.67
  927.8 17.6 %collective-permute-done.68 = bf16[3,4,128,128]{3,0,2,1:T(4,128)(2,1)} collective-permute-done((bf16[3,4,128,128]{3,0,2,1:T(4,128)(2,1)S(1)}, bf16[3,4,128,128]{3,0,2,1:T(4,128)(2,1)}, u32[]{:S(2)}, u32[]{:S(2)}) %collective-permute-start.68) | collective-permute-done | bytes 393248 | tf_op jit(solution)/shard_map/ppermute | solution.py:13
  945.4 153.3 %concatenate.18 = bf16[72,4,128,128]{3,0,2,1:T(8,128)(2,1)} concatenate(bf16[3,4,128,128]{3,0,2,1:T(4,128)(2,1)S(1)} %copy.164, bf16[3,4,128,128]{3,0,2,1:T(4,128)(2,1)S(1)} %collective-permute-done.46, bf16[3,4,128,128]{3,0,2,1:T(4,128)(2,1)S(1)} %collective-permute-done.47, bf16[3,4,128,128]{3,0,2,1:T(4,128)(2,1)S(1)} %collective-permute-done.48, ...), dimensions={0} | concatenate | bytes 18874368 | tf_op jit(solution)/shard_map/concatenate | solution.py:52
  1098.8 78.7 %while.11 = (s32[]{:T(128)}, f32[3,4,128,128]{2,3,1,0:T(8,128)S(1)}, s32[4]{0:T(128)S(1)}, s32[3,32]{1,0:T(4,128)S(1)}, s32[72]{0:T(128)S(1)}, /*index=5*/pred[7...) while((s32[]{:T(128)}, ...), condition=%wide.region_3.4_spmd.clone, body=%wide.region_1.3_spmd.clone.sunk | while | flops 645681728 | bytes 24386944 | solution.py:90
  (248 shorter events, 397.2 us)
Async XLA Ops:
  6.5 1092.2 %all-gather.3.cloned.1.call-start = ((), (), s32[]{:S(2)}) async-start(), calls=%async_computation.1 | async-start | bytes 3538944 | tf_op jit(solution)/shard_map/all_gather | solution.py:36
  24.4 334.5 %collective-permute-start.46 = (bf16[3,4,128,128]{3,0,2,1:T(4,128)(2,1)S(1)}, bf16[3,4,128,128]{3,0,2,1:T(4,128)(2,1)S(1)}, u32[]{:S(2)}, u32[]{:S(2)}) collective-permute-start(bf16[3,4,128,128]{3,0,2,1:T(4,128)(2,1)S(1)} %copy.164), channel_id=1, source_target_pairs={{8,0},{16,8},{24,16},{32,24},{40,32},{48,40},{56,48},{64,56},{72,6... | collective-permute-start | bytes 1179656 | tf_op jit(solution)/shard_map/ppermute | solution.py:13
  28.1 339.7 %collective-permute-start.47 = (bf16[3,4,128,128]{3,0,2,1:T(4,128)(2,1)S(1)}, bf16[3,4,128,128]{3,0,2,1:T(4,128)(2,1)S(1)}, u32[]{:S(2)}, u32[]{:S(2)}) collective-permute-start(bf16[3,4,128,128]{3,0,2,1:T(4,128)(2,1)S(1)} %copy.164), channel_id=1, source_target_pairs={{56,0},{64,8},{72,16},{80,24},{88,32},{96,40},{104,48},{112,56},{1... | collective-permute-start | bytes 1179656 | tf_op jit(solution)/shard_map/ppermute | solution.py:13
  31.9 340.6 %collective-permute-start.48 = (bf16[3,4,128,128]{3,0,2,1:T(4,128)(2,1)S(1)}, bf16[3,4,128,128]{3,0,2,1:T(4,128)(2,1)S(1)}, u32[]{:S(2)}, u32[]{:S(2)}) collective-permute-start(bf16[3,4,128,128]{3,0,2,1:T(4,128)(2,1)S(1)} %copy.164), channel_id=1, source_target_pairs={{64,0},{72,8},{80,16},{88,24},{96,32},{104,40},{112,48},{120,56},{... | collective-permute-start | bytes 1179656 | tf_op jit(solution)/shard_map/ppermute | solution.py:13
  35.2 826.9 %all-to-all-start = ((s32[8,3,4]{2,1,0:T(4,128)}), s32[8,3,4]{2,1,0:T(4,128)S(1)}, u32[]{:S(2)}, u32[]{:S(2)}) async-start(s32[8,3,4]{2,1,0:T(4,128)} %stack.2), calls=%async_computation | async-start | bytes 32768 | tf_op jit(solution)/shard_map/all_to_all | solution.py:32
  54.2 67.9 %collective-permute-start.13 = (s32[3,1]{0,1:T(1,128)}, s32[3,1]{0,1:T(1,128)S(1)}, u32[]{:S(2)}, u32[]{:S(2)}) collective-permute-start(s32[3,1]{0,1:T(1,128)} %param.7), channel_id=1, source_target_pairs={{312,0},{320,8},{328,16},{336,24},{344,32},{352,40},{360,48},{368,... | collective-permute-start | bytes 44 | tf_op jit(solution)/shard_map/ppermute | solution.py:13
  352.5 117.6 %collective-permute-start.50 = (bf16[3,4,128,128]{3,0,2,1:T(4,128)(2,1)S(1)}, bf16[3,4,128,128]{3,0,2,1:T(4,128)(2,1)S(1)}, u32[]{:S(2)}, u32[]{:S(2)}) collective-permute-start(bf16[3,4,128,128]{3,0,2,1:T(4,128)(2,1)S(1)} %copy.164), channel_id=1, source_target_pairs={{120,0},{128,8},{136,16},{144,24},{152,32},{160,40},{168,48},{176,... | collective-permute-start | bytes 1179656 | tf_op jit(solution)/shard_map/ppermute | solution.py:13
  358.9 113.2 %collective-permute-start.51 = (bf16[3,4,128,128]{3,0,2,1:T(4,128)(2,1)S(1)}, bf16[3,4,128,128]{3,0,2,1:T(4,128)(2,1)S(1)}, u32[]{:S(2)}, u32[]{:S(2)}) collective-permute-start(bf16[3,4,128,128]{3,0,2,1:T(4,128)(2,1)S(1)} %copy.164), channel_id=1, source_target_pairs={{128,0},{136,8},{144,16},{152,24},{160,32},{168,40},{176,48},{184,... | collective-permute-start | bytes 1179656 | tf_op jit(solution)/shard_map/ppermute | solution.py:13
  367.8 119.7 %collective-permute-start.52 = (bf16[3,4,128,128]{3,0,2,1:T(4,128)(2,1)S(1)}, bf16[3,4,128,128]{3,0,2,1:T(4,128)(2,1)S(1)}, u32[]{:S(2)}, u32[]{:S(2)}) collective-permute-start(bf16[3,4,128,128]{3,0,2,1:T(4,128)(2,1)S(1)} %copy.164), channel_id=1, source_target_pairs={{136,0},{144,8},{152,16},{160,24},{168,32},{176,40},{184,48},{192,... | collective-permute-start | bytes 1179656 | tf_op jit(solution)/shard_map/ppermute | solution.py:13
  372.5 157.3 %collective-permute-start.53 = (bf16[3,4,128,128]{3,0,2,1:T(4,128)(2,1)S(1)}, bf16[3,4,128,128]{3,0,2,1:T(4,128)(2,1)S(1)}, u32[]{:S(2)}, u32[]{:S(2)}) collective-permute-start(bf16[3,4,128,128]{3,0,2,1:T(4,128)(2,1)S(1)} %copy.164), channel_id=1, source_target_pairs={{184,0},{192,8},{200,16},{208,24},{216,32},{224,40},{232,48},{240,... | collective-permute-start | bytes 1179656 | tf_op jit(solution)/shard_map/ppermute | solution.py:13
  409.3 196.5 %collective-permute-start.54 = (bf16[3,4,128,128]{3,0,2,1:T(4,128)(2,1)S(1)}, bf16[3,4,128,128]{3,0,2,1:T(4,128)(2,1)}, u32[]{:S(2)}, u32[]{:S(2)}) collective-permute-start(bf16[3,4,128,128]{3,0,2,1:T(4,128)(2,1)S(1)} %copy.164), channel_id=1, source_target_pairs={{192,0},{200,8},{208,16},{216,24},{224,32},{232,40},{240,48},{248,... | collective-permute-start | bytes 1179656 | tf_op jit(solution)/shard_map/ppermute | solution.py:13
  470.1 150.7 %collective-permute-start.55 = (bf16[3,4,128,128]{3,0,2,1:T(4,128)(2,1)S(1)}, bf16[3,4,128,128]{3,0,2,1:T(4,128)(2,1)}, u32[]{:S(2)}, u32[]{:S(2)}) collective-permute-start(bf16[3,4,128,128]{3,0,2,1:T(4,128)(2,1)S(1)} %copy.164), channel_id=1, source_target_pairs={{200,0},{208,8},{216,16},{224,24},{232,32},{240,40},{248,48},{256,... | collective-permute-start | bytes 1179656 | tf_op jit(solution)/shard_map/ppermute | solution.py:13
  472.1 162.0 %collective-permute-start.56 = (bf16[3,4,128,128]{3,0,2,1:T(4,128)(2,1)S(1)}, bf16[3,4,128,128]{3,0,2,1:T(4,128)(2,1)}, u32[]{:S(2)}, u32[]{:S(2)}) collective-permute-start(bf16[3,4,128,128]{3,0,2,1:T(4,128)(2,1)S(1)} %copy.164), channel_id=1, source_target_pairs={{248,0},{256,8},{264,16},{272,24},{280,32},{288,40},{296,48},{304,... | collective-permute-start | bytes 1179656 | tf_op jit(solution)/shard_map/ppermute | solution.py:13
  487.5 153.6 %collective-permute-start.57 = (bf16[3,4,128,128]{3,0,2,1:T(4,128)(2,1)S(1)}, bf16[3,4,128,128]{3,0,2,1:T(4,128)(2,1)}, u32[]{:S(2)}, u32[]{:S(2)}) collective-permute-start(bf16[3,4,128,128]{3,0,2,1:T(4,128)(2,1)S(1)} %copy.164), channel_id=1, source_target_pairs={{256,0},{264,8},{272,16},{280,24},{288,32},{296,40},{304,48},{312,... | collective-permute-start | bytes 1179656 | tf_op jit(solution)/shard_map/ppermute | solution.py:13
  529.8 119.0 %collective-permute-start.58 = (bf16[3,4,128,128]{3,0,2,1:T(4,128)(2,1)S(1)}, bf16[3,4,128,128]{3,0,2,1:T(4,128)(2,1)}, u32[]{:S(2)}, u32[]{:S(2)}) collective-permute-start(bf16[3,4,128,128]{3,0,2,1:T(4,128)(2,1)S(1)} %copy.164), channel_id=1, source_target_pairs={{264,0},{272,8},{280,16},{288,24},{296,32},{304,40},{312,48},{320,... | collective-permute-start | bytes 1179656 | tf_op jit(solution)/shard_map/ppermute | solution.py:13
  620.9 112.3 %collective-permute-start.60 = (bf16[3,4,128,128]{3,0,2,1:T(4,128)(2,1)S(1)}, bf16[3,4,128,128]{3,0,2,1:T(4,128)(2,1)}, u32[]{:S(2)}, u32[]{:S(2)}) collective-permute-start(bf16[3,4,128,128]{3,0,2,1:T(4,128)(2,1)S(1)} %copy.164), channel_id=1, source_target_pairs={{320,0},{328,8},{336,16},{344,24},{352,32},{360,40},{368,48},{376,... | collective-permute-start | bytes 1179656 | tf_op jit(solution)/shard_map/ppermute | solution.py:13
  634.1 178.1 %collective-permute-start.61 = (bf16[3,4,128,128]{3,0,2,1:T(4,128)(2,1)S(1)}, bf16[3,4,128,128]{3,0,2,1:T(4,128)(2,1)}, u32[]{:S(2)}, u32[]{:S(2)}) collective-permute-start(bf16[3,4,128,128]{3,0,2,1:T(4,128)(2,1)S(1)} %copy.164), channel_id=1, source_target_pairs={{328,0},{336,8},{344,16},{352,24},{360,32},{368,40},{376,48},{384,... | collective-permute-start | bytes 1179656 | tf_op jit(solution)/shard_map/ppermute | solution.py:13
  641.1 175.3 %collective-permute-start.62 = (bf16[3,4,128,128]{3,0,2,1:T(4,128)(2,1)S(1)}, bf16[3,4,128,128]{3,0,2,1:T(4,128)(2,1)}, u32[]{:S(2)}, u32[]{:S(2)}) collective-permute-start(bf16[3,4,128,128]{3,0,2,1:T(4,128)(2,1)S(1)} %copy.164), channel_id=1, source_target_pairs={{376,0},{384,8},{392,16},{400,24},{408,32},{416,40},{424,48},{432,... | collective-permute-start | bytes 1179656 | tf_op jit(solution)/shard_map/ppermute | solution.py:13
  648.8 184.5 %collective-permute-start.63 = (bf16[3,4,128,128]{3,0,2,1:T(4,128)(2,1)S(1)}, bf16[3,4,128,128]{3,0,2,1:T(4,128)(2,1)}, u32[]{:S(2)}, u32[]{:S(2)}) collective-permute-start(bf16[3,4,128,128]{3,0,2,1:T(4,128)(2,1)S(1)} %copy.164), channel_id=1, source_target_pairs={{384,0},{392,8},{400,16},{408,24},{416,32},{424,40},{432,48},{440,... | collective-permute-start | bytes 1179656 | tf_op jit(solution)/shard_map/ppermute | solution.py:13
  663.1 199.7 %collective-permute-start.64 = (bf16[3,4,128,128]{3,0,2,1:T(4,128)(2,1)S(1)}, bf16[3,4,128,128]{3,0,2,1:T(4,128)(2,1)}, u32[]{:S(2)}, u32[]{:S(2)}) collective-permute-start(bf16[3,4,128,128]{3,0,2,1:T(4,128)(2,1)S(1)} %copy.164), channel_id=1, source_target_pairs={{392,0},{400,8},{408,16},{416,24},{424,32},{432,40},{440,48},{448,... | collective-permute-start | bytes 1179656 | tf_op jit(solution)/shard_map/ppermute | solution.py:13
  733.2 129.7 %collective-permute-start.65 = (bf16[3,4,128,128]{3,0,2,1:T(4,128)(2,1)S(1)}, bf16[3,4,128,128]{3,0,2,1:T(4,128)(2,1)}, u32[]{:S(2)}, u32[]{:S(2)}) collective-permute-start(bf16[3,4,128,128]{3,0,2,1:T(4,128)(2,1)S(1)} %copy.164), channel_id=1, source_target_pairs={{440,0},{448,8},{456,16},{464,24},{472,32},{480,40},{488,48},{496,... | collective-permute-start | bytes 1179656 | tf_op jit(solution)/shard_map/ppermute | solution.py:13
  812.2 105.0 %collective-permute-start.66 = (bf16[3,4,128,128]{3,0,2,1:T(4,128)(2,1)S(1)}, bf16[3,4,128,128]{3,0,2,1:T(4,128)(2,1)}, u32[]{:S(2)}, u32[]{:S(2)}) collective-permute-start(bf16[3,4,128,128]{3,0,2,1:T(4,128)(2,1)S(1)} %copy.164), channel_id=1, source_target_pairs={{448,0},{456,8},{464,16},{472,24},{480,32},{488,40},{496,48},{504,... | collective-permute-start | bytes 1179656 | tf_op jit(solution)/shard_map/ppermute | solution.py:13
  816.4 111.4 %collective-permute-start.67 = (bf16[3,4,128,128]{3,0,2,1:T(4,128)(2,1)S(1)}, bf16[3,4,128,128]{3,0,2,1:T(4,128)(2,1)}, u32[]{:S(2)}, u32[]{:S(2)}) collective-permute-start(bf16[3,4,128,128]{3,0,2,1:T(4,128)(2,1)S(1)} %copy.164), channel_id=1, source_target_pairs={{456,0},{464,8},{472,16},{480,24},{488,32},{496,40},{504,48},{0,56... | collective-permute-start | bytes 1179656 | tf_op jit(solution)/shard_map/ppermute | solution.py:13
  833.3 112.1 %collective-permute-start.68 = (bf16[3,4,128,128]{3,0,2,1:T(4,128)(2,1)S(1)}, bf16[3,4,128,128]{3,0,2,1:T(4,128)(2,1)}, u32[]{:S(2)}, u32[]{:S(2)}) collective-permute-start(bf16[3,4,128,128]{3,0,2,1:T(4,128)(2,1)S(1)} %copy.164), channel_id=1, source_target_pairs={{504,0},{0,8},{8,16},{16,24},{24,32},{32,40},{40,48},{48,56},{56,6... | collective-permute-start | bytes 1179656 | tf_op jit(solution)/shard_map/ppermute | solution.py:13
  (76 other events, 11497.3 us)
Sparse Core Ops, SparseCore 0:
  10.6 81.3 all-gather.2
